TPU v7x, 512 devices: a whole 4x8x8 slice. The times are simulated.
512 devices in a mesh: blk: 256 (over x_lo, y, z, core), rep: 2 (over x_hi).
Axes of the slice: x: 4 (x_hi: 2, x_lo: 2; x = x_hi * 2 + x_lo), y: 8, z: 8, core: 2. Of those that a mesh axis runs over, the one named last changes fastest.
Arguments:
- images: bfloat16 [2, 131072, 1152], P('rep', 'blk'), may hold values from -96 to 96
- texts: bfloat16 [2, 131072, 1152], P('rep', 'blk'), may hold values from -96 to 96
- labels: int32 [2, 131072], P('rep', 'blk'), may hold values from 0 to 131071, as said below
- log_temp: float32 [1], replicated, may hold values from 4.2 to 4.6
- bias: float32 [1], replicated, may hold values from -14 to -11
Outputs:
- grad_images: bfloat16 [2, 131072, 1152], P('rep', 'blk')
- grad_texts: bfloat16 [2, 131072, 1152], P('rep', 'blk')
- stats: float32 [3], replicated
Inputs may be any that keep to these rules, and one draw needn't show every extreme that they name: labels[g, i] lies in text block (i // 512 - r) mod (256) for some r with 0 <= r < 4.
All inputs are finite; a program needn't handle non-finite values.
Results may differ from a plain program's by a relative error of at most 0.0065.
Values may be sent and summed in bfloat16 or wider, within the bound.
A program may use at most 64 MiB of HBM per device.

v0:
```python
import jax
import jax.numpy as jnp
from jax import lax
from jax.sharding import PartitionSpec as P

ROUNDS = 4


EPS = 1e-06


def passed_along(value, axis, steps):
    count = lax.axis_size(axis)
    pairs = [(source, (source + steps) % count) for source in range(count)]
    return lax.ppermute(value, axis, pairs)


def normalize(rows):
    rows32 = rows.astype(jnp.float32)
    rinv = lax.rsqrt(jnp.sum(rows32 * rows32, axis=-1, keepdims=True) + EPS)
    return (rows32 * rinv, rinv)


def project_back(grad, unit, rinv):
    return ((grad - unit * jnp.sum(unit * grad, axis=-1, keepdims=True)) * rinv).astype(
        jnp.bfloat16
    )


def block_scores(img_unit, txt_unit, img_labels, text_first, temp, shift_b):
    count = txt_unit.shape[0]
    scaled = temp * lax.dot_general(
        img_unit, txt_unit, (((1,), (1,)), ((), ())), preferred_element_type=jnp.float32
    )
    ident = text_first + jnp.arange(count, dtype=jnp.int32)
    sign = jnp.where(img_labels[:, None] == ident[None, :], 1.0, -1.0).astype(jnp.float32)
    logit = scaled + shift_b
    slope = -sign * jax.nn.sigmoid(-sign * logit)
    totals = jnp.stack(
        [jnp.sum(-jax.nn.log_sigmoid(sign * logit)), jnp.sum(slope * scaled), jnp.sum(slope)]
    )
    weight = (temp * slope).astype(jnp.bfloat16)
    img_term = jnp.dot(weight, txt_unit, preferred_element_type=jnp.float32)
    return (weight, img_term, totals)


def text_term(weight, img_unit):
    return lax.dot_general(
        weight, img_unit, (((0,), (0,)), ((), ())), preferred_element_type=jnp.float32
    )


def shards(images, texts, labels, log_temp, bias):
    temp = jnp.exp(log_temp[0])
    shift_b = bias[0]
    xn32, rinv_x = normalize(images[0])
    yn32, rinv_y = normalize(texts[0])
    xn = xn32.astype(jnp.bfloat16)
    yn = yn32.astype(jnp.bfloat16)
    own_labels = labels[0]
    rows = xn.shape[0]
    place = lax.axis_index("blk")
    blocks = lax.axis_size("blk")
    weight, grad_x, totals = block_scores(xn, yn, own_labels, place * rows, temp, shift_b)
    own_text = text_term(weight, xn)
    text_rounds = ROUNDS - 1
    moving = yn
    partial_value = own_text
    for offset in range(1, text_rounds + 1):
        moving, partial_value = (
            passed_along(moving.astype(jnp.float32), "blk", 1).astype(moving.dtype),
            passed_along(partial_value, "blk", 1),
        )
        owner = (place - offset) % blocks
        weight, img_term, extra = block_scores(xn, moving, own_labels, owner * rows, temp, shift_b)
        grad_x = grad_x + img_term
        partial_value = partial_value + text_term(weight, xn)
        totals = totals + extra
    grad_y = passed_along(partial_value, "blk", -text_rounds)
    summed = lax.psum(totals, ("blk", "rep"))
    stats = summed / jnp.float32(blocks * lax.axis_size("rep") * rows)
    return (
        project_back(grad_x, xn32, rinv_x)[None],
        project_back(grad_y, yn32, rinv_y)[None],
        stats,
    )


def solution(mesh):
    return jax.shard_map(
        shards,
        mesh=mesh,
        in_specs=(P("rep", "blk", None), P("rep", "blk", None), P("rep", "blk"), P(), P()),
        out_specs=(P("rep", "blk", None), P("rep", "blk", None), P()),
        check_vma=False,
    )
```

profile of v0, /device:TPU:1, one launch (start us, length us, event | category | flops | bytes accessed | tf_op | source)
XLA Modules:
  0.0 339.9 jit_solution(11024422725717898739)
XLA Ops:
  0.6 0.0 copy-start.1
  0.6 0.0 copy-start
  0.7 1.7 fusion.15
  2.4 1.6 fusion.21
  5.3 0.0 copy-done.1
  5.4 0.0 copy-done
  5.4 0.0 copy-start.7
  5.4 1.0 convolution_multiply_fusion.3
  6.3 0.0 copy-start.17
  6.4 0.0 copy-done.7
  6.4 2.6 fusion.69
  9.0 0.0 copy-done.17
  9.0 5.4 %collective-permute-start.3 = (f32[512,1152]{1,0:T(8,128)}, f32[512,1152]{1,0:T(8,128)}, u32[]{:S(2)}, u32[]{:S(2)}) collective-permute-start(f32[512,1152]{1,0:T(8,128)} %fusion.69), channel_id=1, source_target_pairs={{0,2},{2,4},{4,6},{6,8},{8,10},{10,12},{12,14},{14,16},{16,18},{18... | collective-permute-start | bytes 7077896 | tf_op jit(solution)/shard_map/ppermute | solution.py:15
  14.4 0.3 fusion.66
  14.7 1.9 collective-permute-start
  16.6 36.4 %collective-permute-done = bf16[512,1152]{1,0:T(8,128)(2,1)} collective-permute-done((bf16[512,1152]{1,0:T(8,128)(2,1)S(1)}, bf16[512,1152]{1,0:T(8,128)(2,1)}, u32[]{:S(2)}, u32[]{:S(2)}) %collective-permute-start) | collective-permute-done | bytes 1179680 | tf_op jit(solution)/shard_map/ppermute | solution.py:15
  53.0 2.2 convolution_multiply_fusion.2
  55.2 0.0 copy-start.11
  55.2 0.0 collective-permute-done.3
  55.2 4.7 %convolution_add_fusion = f32[512,1152]{1,0:T(8,128)} fusion(f32[512,1152]{1,0:T(8,128)} %collective-permute-done.3, f32[]{:T(128)} %bitcast, bf16[1,512,1152]{2,1,0:T(8,128)(2,1)S(1)} %copy-done.1, f32[512]{0:T(512)S(1)} %add_rsqrt_fusion.1, f32[512,512]{1,0:T(8,128)S(1)} %convolution_multiply_fusion.2, s32[512]{0:T(512)S(1)} %iota_add_fusion.2, ...), kind=kOutput, calls=%fused_computation | convolution fusion | flops 609222656 | bytes 6952968 | tf_op jit(solution)/shard_map/dot_general | solution.py:48
  59.9 4.6 %collective-permute-start.4 = (f32[512,1152]{1,0:T(8,128)}, f32[512,1152]{1,0:T(8,128)}, u32[]{:S(2)}, u32[]{:S(2)}) collective-permute-start(f32[512,1152]{1,0:T(8,128)} %convolution_add_fusion), channel_id=1, source_target_pairs={{0,2},{2,4},{4,6},{6,8},{8,10},{10,12},{12,14},{14,16},{16,18},{18... | collective-permute-start | bytes 7077896 | tf_op jit(solution)/shard_map/ppermute | solution.py:15
  64.5 1.9 collective-permute-start.1
  66.5 0.0 copy-start.3
  66.5 36.8 %collective-permute-done.1 = bf16[512,1152]{1,0:T(8,128)(2,1)} collective-permute-done((bf16[512,1152]{1,0:T(8,128)(2,1)}, bf16[512,1152]{1,0:T(8,128)(2,1)}, u32[]{:S(2)}, u32[]{:S(2)}) %collective-permute-start.1) | collective-permute-done | bytes 1179680 | tf_op jit(solution)/shard_map/ppermute | solution.py:15
  103.2 4.4 %collective-permute-start.2 = (bf16[512,1152]{1,0:T(8,128)(2,1)}, bf16[512,1152]{1,0:T(8,128)(2,1)}, u32[]{:S(2)}, u32[]{:S(2)}) collective-permute-start(bf16[512,1152]{1,0:T(8,128)(2,1)} %collective-permute-done.1), channel_id=1, source_target_pairs={{0,2},{2,4},{4,6},{6,8},{8,10},{10,12},{12,14},{14,16},{16,18},{18... | collective-permute-start | bytes 3538952 | tf_op jit(solution)/shard_map/ppermute | solution.py:15
  107.6 2.2 convolution_multiply_fusion.1
  109.8 0.0 copy-start.13
  109.8 0.0 copy-done.8
  109.8 1.2 fusion.70
  111.0 0.0 copy-done.13
  111.0 0.0 collective-permute-done.4
  111.0 3.5 %add.168 = f32[512,1152]{1,0:T(8,128)} add(f32[512,1152]{1,0:T(8,128)} %collective-permute-done.4, f32[512,1152]{1,0:T(8,128)S(1)} %fusion.70) | non-fusion elementwise | flops 589824 | bytes 7077888 | tf_op jit(solution)/shard_map/add | solution.py:77
  114.5 2.1 collective-permute-start.5
  116.6 0.0 copy-start.5
  116.6 0.0 copy-start.14
  116.6 0.0 copy-start.18
  116.6 2.6 fusion.67
  119.3 3.8 %collective-permute-done.2 = bf16[512,1152]{1,0:T(8,128)(2,1)} collective-permute-done((bf16[512,1152]{1,0:T(8,128)(2,1)}, bf16[512,1152]{1,0:T(8,128)(2,1)}, u32[]{:S(2)}, u32[]{:S(2)}) %collective-permute-start.2) | collective-permute-done | bytes 1179680 | tf_op jit(solution)/shard_map/ppermute | solution.py:15
  123.1 0.0 copy-done.11
  123.1 0.0 copy-done.3
  123.1 0.0 copy-done.14
  123.1 0.0 copy-done.18
  123.1 8.3 %fusion.62 = (f32[]{:T(128)}, f32[]{:T(128)}, f32[]{:T(128)}, f32[]{:T(128)}, f32[]{:T(128)}, /*index=5*/f32[]{:T(128)}, f32[]{:T(128)}, f32[]{:T(128)}, f32[]{:...) fusion(s32[512]{0:T(512)S(1)} %iota_add_fusion, f32[]{:T(128)} %bitcast.95, s32[512]{0:T(512)S(1)} %bitcast.105, ...), kind=kOutput, calls=%fused_computation.83 | convolution fusion | flops 628031488 | bytes 6565944 | tf_op jit(solution)/shard_map/dot_general | solution.py:32
  131.4 0.0 copy-done.5
  131.4 2.4 fusion.71
  133.8 0.0 copy-start.9
  133.8 0.0 copy-start.12
  133.9 12.5 %collective-permute-done.5 = f32[512,1152]{1,0:T(8,128)} collective-permute-done((f32[512,1152]{1,0:T(8,128)}, f32[512,1152]{1,0:T(8,128)}, u32[]{:S(2)}, u32[]{:S(2)}) %collective-permute-start.5) | collective-permute-done | bytes 2359328 | tf_op jit(solution)/shard_map/ppermute | solution.py:15
  146.3 3.5 %add.169 = f32[512,1152]{1,0:T(8,128)} add(f32[512,1152]{1,0:T(8,128)} %collective-permute-done.5, f32[512,1152]{1,0:T(8,128)S(1)} %fusion.71) | non-fusion elementwise | flops 589824 | bytes 7077888 | tf_op jit(solution)/shard_map/add | solution.py:77
  149.8 14.9 %collective-permute-start.6 = (f32[512,1152]{1,0:T(8,128)}, f32[512,1152]{1,0:T(8,128)S(1)}, u32[]{:S(2)}, u32[]{:S(2)}) collective-permute-start(f32[512,1152]{1,0:T(8,128)} %add.169), channel_id=1, source_target_pairs={{0,506},{2,508},{4,510},{6,0},{8,2},{10,4},{12,6},{14,8},{16,10},{... | collective-permute-start | bytes 7077896 | tf_op jit(solution)/shard_map/ppermute | solution.py:15
  164.7 8.2 %fusion.73 = f32[3]{0:T(128)} fusion(f32[1]{0:T(128)} %bitcast.11, f32[1]{0:T(128)} %bitcast.10, f32[1]{0:T(128)} %bitcast.9, f32[1]{0:T(128)} %bitcast.14, f32[1]{0:T(128)} %bitcast.13, f32[1]{0:T(128)} %bitcast.12, f32[1]{0:T(128)} %bitcast.17, f32[1]{0:T(128)} %bitcast.16, f32[1]{0:T(128)} %bitcast.15, f32[1]{0:T(128)} %bitcast.20, f32[1]{0:T(128)} %bitcast.19, ...), kind=kLoop, calls=%fused_computation.108 | loop fusion | flops 33 | bytes 60 | tf_op jit(solution)/shard_map/add | solution.py:78
  172.9 0.0 copy-done.9
  172.9 0.0 copy-done.12
  172.9 3.9 %convolution_add_fusion.2 = f32[512,1152]{1,0:T(8,128)} fusion(f32[512,1152]{1,0:T(8,128)S(1)} %fusion.67, f32[]{:T(128)} %bitcast, bf16[512,1152]{1,0:T(8,128)(2,1)} %collective-permute-done, f32[512,512]{1,0:T(8,128)S(1)} %copy-done.12, s32[512]{0:T(512)S(1)} %iota_add_fusion.2, f32[]{:T(128)} %bitcast.98, s32[512]{0:T(512)S(1)} %bitcast.107), kind=kOutput, calls=%fused_computation.2 | convolution fusion | flops 607453184 | bytes 6950920 | tf_op jit(solution)/shard_map/dot_general | solution.py:43
  176.8 153.4 %psum.7 = f32[3]{0:T(128)S(1)} all-reduce(f32[3]{0:T(128)} %fusion.73), channel_id=1, replica_groups=mesh['blk'=256,'rep'=2] {'blk','rep'}, use_global_device_ids=true, to_apply=%region_16.17 | all-reduce | flops 3 | bytes 24 | tf_op jit(solution)/shard_map/psum | solution.py:80
  330.2 0.5 broadcast_multiply_fusion
  330.7 0.0 copy-start.15
  330.7 2.9 fusion.63
  333.7 0.0 copy-done.16
  333.8 2.7 fusion.11
  336.5 1.5 fusion.36
  338.0 0.0 collective-permute-done.6
  338.0 0.4 fusion.17
  338.4 1.5 fusion.33
  (17 shorter events, 0.0 us)
Async XLA Ops:
  0.6 4.7 %copy-start.1 = (bf16[1,512,1152]{2,1,0:T(8,128)(2,1)S(1)}, bf16[1,512,1152]{2,1,0:T(8,128)(2,1)}, u32[]{:S(2)}) copy-start(bf16[1,512,1152]{2,1,0:T(8,128)(2,1)} %param.5) | copy-start | bytes 3538948
  0.6 4.7 %copy-start = (bf16[1,512,1152]{2,1,0:T(8,128)(2,1)S(1)}, bf16[1,512,1152]{2,1,0:T(8,128)(2,1)}, u32[]{:S(2)}) copy-start(bf16[1,512,1152]{2,1,0:T(8,128)(2,1)} %param.6) | copy-start | bytes 3538948
  5.4 1.0 copy-start.7
  6.3 2.7 copy-start.17
  9.0 46.2 %collective-permute-start.3 = (f32[512,1152]{1,0:T(8,128)}, f32[512,1152]{1,0:T(8,128)}, u32[]{:S(2)}, u32[]{:S(2)}) collective-permute-start(f32[512,1152]{1,0:T(8,128)} %fusion.69), channel_id=1, source_target_pairs={{0,2},{2,4},{4,6},{6,8},{8,10},{10,12},{12,14},{14,16},{16,18},{18... | collective-permute-start | bytes 7077896 | tf_op jit(solution)/shard_map/ppermute | solution.py:15
  14.7 38.3 %collective-permute-start = (bf16[512,1152]{1,0:T(8,128)(2,1)S(1)}, bf16[512,1152]{1,0:T(8,128)(2,1)}, u32[]{:S(2)}, u32[]{:S(2)}) collective-permute-start(bf16[512,1152]{1,0:T(8,128)(2,1)S(1)} %fusion.66), channel_id=1, source_target_pairs={{0,2},{2,4},{4,6},{6,8},{8,10},{10,12},{12,14},{14,16},{16,18},{18... | collective-permute-start | bytes 3538952 | tf_op jit(solution)/shard_map/ppermute | solution.py:15
  55.2 67.9 %copy-start.11 = (f32[512,512]{1,0:T(8,128)}, f32[512,512]{1,0:T(8,128)S(1)}, u32[]{:S(2)}) copy-start(f32[512,512]{1,0:T(8,128)S(1)} %convolution_multiply_fusion.2) | copy-start | bytes 3145732
  59.9 49.9 %copy-start.8 = (s32[1,512]{1,0:T(1,128)S(1)}, s32[1,512]{1,0:T(1,128)}, u32[]{:S(2)}) copy-start(s32[1,512]{1,0:T(1,128)} %param.7) | copy-start | bytes 6148
  59.9 51.1 %collective-permute-start.4 = (f32[512,1152]{1,0:T(8,128)}, f32[512,1152]{1,0:T(8,128)}, u32[]{:S(2)}, u32[]{:S(2)}) collective-permute-start(f32[512,1152]{1,0:T(8,128)} %convolution_add_fusion), channel_id=1, source_target_pairs={{0,2},{2,4},{4,6},{6,8},{8,10},{10,12},{12,14},{14,16},{16,18},{18... | collective-permute-start | bytes 7077896 | tf_op jit(solution)/shard_map/ppermute | solution.py:15
  64.5 38.7 %collective-permute-start.1 = (bf16[512,1152]{1,0:T(8,128)(2,1)}, bf16[512,1152]{1,0:T(8,128)(2,1)}, u32[]{:S(2)}, u32[]{:S(2)}) collective-permute-start(bf16[512,1152]{1,0:T(8,128)(2,1)} %collective-permute-done), channel_id=1, source_target_pairs={{0,2},{2,4},{4,6},{6,8},{8,10},{10,12},{12,14},{14,16},{16,18},{18... | collective-permute-start | bytes 3538952 | tf_op jit(solution)/shard_map/ppermute | solution.py:15
  66.5 56.6 %copy-start.3 = (s32[512]{0:T(512)}, s32[512]{0:T(512)S(1)}, u32[]{:S(2)}) copy-start(s32[512]{0:T(512)S(1)} %iota_add_fusion.1) | copy-start | bytes 6148
  103.2 19.9 %collective-permute-start.2 = (bf16[512,1152]{1,0:T(8,128)(2,1)}, bf16[512,1152]{1,0:T(8,128)(2,1)}, u32[]{:S(2)}, u32[]{:S(2)}) collective-permute-start(bf16[512,1152]{1,0:T(8,128)(2,1)} %collective-permute-done.1), channel_id=1, source_target_pairs={{0,2},{2,4},{4,6},{6,8},{8,10},{10,12},{12,14},{14,16},{16,18},{18... | collective-permute-start | bytes 3538952 | tf_op jit(solution)/shard_map/ppermute | solution.py:15
  109.8 1.2 copy-start.13
  114.5 31.9 %collective-permute-start.5 = (f32[512,1152]{1,0:T(8,128)}, f32[512,1152]{1,0:T(8,128)}, u32[]{:S(2)}, u32[]{:S(2)}) collective-permute-start(f32[512,1152]{1,0:T(8,128)} %add.168), channel_id=1, source_target_pairs={{0,2},{2,4},{4,6},{6,8},{8,10},{10,12},{12,14},{14,16},{16,18},{18... | collective-permute-start | bytes 7077896 | tf_op jit(solution)/shard_map/ppermute | solution.py:15
  116.6 14.8 %copy-start.5 = (s32[512]{0:T(512)}, s32[512]{0:T(512)S(1)}, u32[]{:S(2)}) copy-start(s32[512]{0:T(512)S(1)} %iota_add_fusion) | copy-start | bytes 6148
  116.6 6.5 %copy-start.14 = (f32[512,512]{1,0:T(8,128)S(1)}, f32[512,512]{1,0:T(8,128)}, u32[]{:S(2)}) copy-start(f32[512,512]{1,0:T(8,128)} %copy-done.13) | copy-start | bytes 3145732
  116.6 6.5 %copy-start.18 = (f32[512,512]{1,0:T(8,128)S(1)}, f32[512,512]{1,0:T(8,128)}, u32[]{:S(2)}) copy-start(f32[512,512]{1,0:T(8,128)} %copy-done.17) | copy-start | bytes 3145732
  133.8 39.1 %copy-start.9 = (s32[1,512]{1,0:T(1,128)S(1)}, s32[1,512]{1,0:T(1,128)}, u32[]{:S(2)}) copy-start(s32[1,512]{1,0:T(1,128)} %param.7) | copy-start | bytes 6148
  133.8 39.1 %copy-start.12 = (f32[512,512]{1,0:T(8,128)S(1)}, f32[512,512]{1,0:T(8,128)}, u32[]{:S(2)}) copy-start(f32[512,512]{1,0:T(8,128)} %copy-done.11) | copy-start | bytes 3145732
  149.8 188.2 %collective-permute-start.6 = (f32[512,1152]{1,0:T(8,128)}, f32[512,1152]{1,0:T(8,128)S(1)}, u32[]{:S(2)}, u32[]{:S(2)}) collective-permute-start(f32[512,1152]{1,0:T(8,128)} %add.169), channel_id=1, source_target_pairs={{0,506},{2,508},{4,510},{6,0},{8,2},{10,4},{12,6},{14,8},{16,10},{... | collective-permute-start | bytes 7077896 | tf_op jit(solution)/shard_map/ppermute | solution.py:15
  172.9 157.8 %copy-start.6 = (s32[512]{0:T(512)S(1)}, s32[512]{0:T(512)}, u32[]{:S(2)}) copy-start(s32[512]{0:T(512)} %copy-done.5) | copy-start | bytes 6148
  330.7 3.0 copy-start.2
  330.7 3.0 copy-start.4
  330.7 3.0 copy-start.10
  330.7 3.0 copy-start.15
  330.7 3.0 copy-start.16
where the time goes:
time: 341 us; the launch traced here: 340 us
  blocking collectives  153 us (45%)
  waiting for transfers between devices  89.5 us (26%)
  matrix products  36.7 us (11%)
  starting transfers between devices  35.2 us (10%)
  other arithmetic  22.7 us (7%)
    psum x1, blocking collectives, shards(): summed = lax.psum(totals, ('blk', 'rep'))  153 us
    ppermute x7, waiting for transfers between devices, passed_along(): return lax.ppermute(value, axis, pairs)  89.5 us
    ppermute x7, starting transfers between devices, passed_along(): return lax.ppermute(value, axis, pairs)  35.2 us
    dot_general x4, matrix products, block_scores(): lax.dot_general(img_unit, txt_unit, (((1,), (1,)), ((), ())), preferred_e...  13.6 us
    dot_general x4, matrix products, block_scores(): img_term = jnp.dot(weight, txt_unit, preferred_element_type=jnp.float32)  12.2 us
    dot_general x4, matrix products, text_term(): lax.dot_general(weight, img_unit, (((0,), (0,)), ((), ())), preferred_ele...  10.9 us
    add x1, other arithmetic, shards(): totals = totals + extra  8.21 us
    add x2, other arithmetic, shards(): partial_value = partial_value + text_term(weight, xn)  6.94 us
  transfers between devices with their start and end apart: 7, of which 4 were waited for; matrix products, arithmetic and copies ran while one was open for 12% of the time, Pallas kernels for 0%

commit v1 on v0

v1 whole, which is shorter than its diff:
```python
import functools

import jax
import jax.numpy as jnp
from jax import lax
from jax.experimental import pallas as pl
from jax.experimental.pallas import tpu as pltpu
from jax.sharding import PartitionSpec as P

MESH = pl.DeviceIdType.MESH
EPS = 1e-06
F32 = jnp.float32
BF16 = jnp.bfloat16
ROWS = 512
D = 1152
CH = 64
NCH = ROWS // CH
ZS, YS, XS = 8, 8, 2


def kernel(blocks, reps, images, texts, labels, log_temp, bias, o_img, o_txt, o_stats,
           buf, raw, acc, rinv, rowv, colv, consts, sbuf, st, arbuf,
           ld, ldl, zs, zr, ps, pr, f1s, f1r, f3s, f3r, fas, far_r, ls, lr,
           os_, or_, bs_, br, ars, arr, rdy, fargo):
    me = lax.axis_index("blk")
    rep = lax.axis_index("rep")
    core = lax.rem(me, 2)
    F = core
    N = 1 - core
    sgn = 2 * core - 1

    def at(step):
        return lax.rem(me + step + blocks, blocks)

    peer, far = at(-sgn), at(sgn)
    even, odd = core == 0, core == 1
    z = lax.rem(me // 2, ZS)
    y = lax.rem(me // (2 * ZS), YS)
    x = me // (2 * ZS * YS)
    xi = x * reps + rep

    def x_mate(j):
        i = lax.rem(xi + j, XS * reps)
        return {"blk": me + (i // reps - x) * (2 * ZS * YS), "rep": lax.rem(i, reps)}

    def y_mate(j):
        return {"blk": me + (lax.rem(y + j, YS) - y) * (2 * ZS)}

    def z_mate(j):
        return {"blk": me + (lax.rem(z + j, ZS) - z) * 2}

    groups = [(XS * reps, xi, x_mate), (YS, y, y_mate), (ZS, z, z_mate)]

    bar = pltpu.get_barrier_semaphore()

    def hello(step):
        pl.semaphore_signal(bar, inc=1, device_id={"blk": at(step)}, device_id_type=MESH)

    hello(2)
    hello(-2)

    @pl.when(odd)
    def _():
        for step in (1, -1, 3, -3):
            hello(step)

    @pl.when(even)
    def _():
        for size, _, mate in groups:
            for j in range(1, size):
                pl.semaphore_signal(bar, inc=1, device_id=mate(j), device_id_type=MESH)

    LB = 128
    srcs = (images, texts)

    def load(f, j):
        s = pl.ds(j * LB, LB)
        return pltpu.make_async_copy(srcs[f].at[0, s], raw.at[f, s], ld.at[f, j])

    for j in range(ROWS // LB):
        for f in (0, 1):
            load(f, j).start()
    lab_load = pltpu.make_async_copy(labels, rowv.at[1, 0], ldl)
    lab_load.start()

    def z_send(f, k):
        s = pl.ds(k * CH, CH)
        return pltpu.make_async_remote_copy(
            src_ref=buf.at[f, 0, s], dst_ref=buf.at[f, 2, s], send_sem=zs.at[f, k], recv_sem=zr.at[f, k],
            device_id={"blk": at(4 * f - 2)}, device_id_type=MESH)

    def peer_send(j):
        s = pl.ds(j * LB, LB)
        return pltpu.make_async_remote_copy(
            src_ref=buf.at[N, 0, s], dst_ref=buf.at[N, 1, s], send_sem=ps.at[j], recv_sem=pr.at[j],
            device_id={"blk": peer}, device_id_type=MESH)

    def pass_on(f, slot_to, k, ss, rs, to):
        s = pl.ds(k * CH, CH)
        return pltpu.make_async_remote_copy(
            src_ref=buf.at[f, 2, s], dst_ref=buf.at[f, slot_to, s], send_sem=ss.at[k], recv_sem=rs.at[k],
            device_id={"blk": to}, device_id_type=MESH)

    def fwd_f(k):
        return pass_on(F, 1, k, f1s, f1r, peer)

    def fwd_n(k):
        return pass_on(N, 3, k, f3s, f3r, peer)

    def far_send(k):
        return pass_on(F, 3, k, fas, far_r, far)

    for j in range(ROWS // LB):
        for f in (0, 1):
            load(f, j).wait()
            s = slice(j * LB, (j + 1) * LB)
            x32 = raw[f, s, :].astype(F32)
            r = lax.rsqrt(jnp.sum(x32 * x32, axis=-1, keepdims=True) + EPS)
            buf[f, 0, s, :] = (x32 * r).astype(BF16)
            rinv[f, s, :] = jnp.broadcast_to(r, (LB, 128))
        if j == 0:

            @pl.when(even)
            def _():
                pl.semaphore_wait(bar, 6 + sum(size - 1 for size, _, _ in groups))
                for step in (1, -1, 3, -3):
                    pl.semaphore_signal(rdy, inc=1, device_id={"blk": at(step)}, device_id_type=MESH)

            @pl.when(odd)
            def _():
                pl.semaphore_wait(bar, 2)

        for k in range(j * LB // CH, (j + 1) * LB // CH):
            for f in (0, 1):
                z_send(f, k).start()

    lab_load.wait()

    def lab_send(r):
        return pltpu.make_async_remote_copy(
            src_ref=rowv.at[1, 0], dst_ref=rowv.at[1, r], send_sem=ls.at[r - 1], recv_sem=lr.at[r - 1],
            device_id={"blk": at(-r)}, device_id_type=MESH)

    @pl.when(odd)
    def _():
        pl.semaphore_wait(rdy, 4)

    for j in range(ROWS // LB):
        peer_send(j).start()
    for r in (1, 2, 3):
        lab_send(r).start()

    lane = lax.broadcasted_iota(jnp.int32, (1, ROWS), 1)
    for r in range(4):
        rowv[0, r] = lane + at(-r) * ROWS
    colv[0] = jnp.transpose(jnp.broadcast_to(rowv[1, 0].astype(F32), (128, ROWS))).astype(jnp.int32)
    colv[1] = lax.broadcasted_iota(jnp.int32, (ROWS, 128), 0) + me * ROWS
    consts[0] = jnp.exp(jnp.full((1, 256), log_temp[0], F32))
    consts[1] = jnp.full((1, 256), bias[0], F32)
    st[...] = jnp.zeros_like(st)

    def clear(i, _):
        for f in (0, 1):
            acc[f, pl.ds(pl.multiple_of(i * 64, 64), 64), :] = jnp.zeros((64, D), F32)
        return 0

    lax.fori_loop(0, ROWS // 64, clear, 0)

    def matches(f, rb, rows, r, c0, width, shift):
        ids = colv[f, rb:rb + rows, :]
        ids = jnp.concatenate([ids] * (width // 128), axis=1) if width > 128 else ids
        return ids == rowv[f, r, :, pl.ds(c0, width)] - shift

    def item(f, own, r, c0, width, flag=None, shift=0, grad=True):
        RB = 256
        for rb in range(0, ROWS, RB):
            other = buf[1 - f, r, pl.ds(c0, width), :]
            scaled = consts[0, :, :width] * lax.dot_general(
                buf[f, own, rb:rb + RB, :], other, (((1,), (1,)), ((), ())), preferred_element_type=F32)
            if flag is not None:
                sbuf[rb:rb + RB, :width] = scaled
            if grad:
                logit = scaled + consts[1, :, :width]
                m = matches(f, rb, RB, r, c0, width, shift)
                sig = 1.0 / (1.0 + jnp.exp(jnp.where(m, logit, -logit)))
                w = (consts[0, :, :width] * jnp.where(m, -sig, sig)).astype(BF16)
                acc[f, rb:rb + RB, :] += jnp.dot(w, other, preferred_element_type=F32)
        if flag is None:
            return

        @pl.when(flag)
        def _():
            SB = 64
            tot = [jnp.zeros((8, 128), F32)] * 3
            for rb in range(0, ROWS, SB):
                scaled = sbuf[rb:rb + SB, :width]
                logit = scaled + consts[1, :, :width]
                m = matches(f, rb, SB, r, c0, width, shift)
                u = jnp.where(m, logit, -logit)
                e = jnp.exp(-jnp.abs(u))
                inv = 1.0 / (1.0 + e)
                sig = jnp.where(u >= 0, e * inv, inv)
                g = jnp.where(m, -sig, sig)
                loss = jnp.maximum(-u, 0.0) + jnp.log1p(e)
                for i, v in enumerate((loss, g * scaled, g)):
                    v = jnp.sum(v.reshape(SB // 8, 8, width), axis=0)
                    for c in range(0, width, 128):
                        tot[i] = tot[i] + v[:, c:c + 128]
            for i in range(3):
                st[i] += tot[i]

    def counted(f, r):
        return jnp.logical_and(f == 0, jnp.logical_or(odd, r < 3))

    def early(i, _):
        r = i // 4
        f = jnp.where(r == 0, i // 2, N)
        h = lax.rem(i, 2)

        @pl.when(i == 4)
        def _():
            for r_ in (1, 2, 3):
                lab_send(r_).wait_recv()
            for j in range(ROWS // LB):
                peer_send(j).wait_recv()

        item(f, 0, r, pl.multiple_of(h * 256, 256), 256, counted(f, r))
        return 0

    lax.fori_loop(0, 6, early, 0)

    def near(q, _):
        for j in (0, 1):
            k = 2 * q + j
            z_send(F, k).wait_recv()
            fwd_f(k).start()
            z_send(N, k).wait_recv()
            fwd_n(k).start()

            @pl.when(q == 3)
            def _():
                if j == 0:
                    def sent(k_, _):
                        z_send(N, k_).wait_send()
                        return 0

                    lax.fori_loop(0, 6, sent, 0)
                    pl.semaphore_signal(fargo, inc=1, device_id={"blk": peer}, device_id_type=MESH)
                    pl.semaphore_wait(fargo, 1)

                def go(k_, _):
                    far_send(k_).start()
                    return 0

                lax.fori_loop(4 * j, 4 * j + 4, go, 0)

        def sub(i, _):
            side = jnp.logical_or(i == 0, i == 3)
            f = jnp.where(side, N, F)
            r = jnp.where(i < 2, 2, jnp.where(i == 2, 1, 3))

            @pl.when(i == 2)
            def _():
                for j in (0, 1):
                    fwd_f(2 * q + j).wait_recv()
                    fwd_n(2 * q + j).wait_recv()

            item(f, 0, r, pl.multiple_of(q * 128, 128), 128, counted(f, r))
            return 0

        lax.fori_loop(0, 4, sub, 0)
        return 0

    lax.fori_loop(0, 4, near, 0)

    @pl.when(even)
    def _():
        def both(h, _):
            item(1, 1, 2, pl.multiple_of(h * 256, 256), 256, flag=h >= 0, shift=(at(-1) - me) * ROWS, grad=False)
            return 0

        lax.fori_loop(0, 2, both, 0)

    row = lax.broadcasted_iota(jnp.int32, (8, 128), 0)
    tile = jnp.zeros((8, 128), F32)
    for i in range(3):
        tile = jnp.where(row == i, jnp.broadcast_to(jnp.sum(st[i], axis=0, keepdims=True), (8, 128)), tile)

    up = pltpu.make_async_remote_copy(
        src_ref=arbuf.at[3, 2], dst_ref=arbuf.at[3, 0], send_sem=os_, recv_sem=or_, device_id={"blk": peer},
        device_id_type=MESH)
    down = pltpu.make_async_remote_copy(
        src_ref=arbuf.at[3, 2], dst_ref=arbuf.at[3, 1], send_sem=bs_, recv_sem=br, device_id={"blk": peer},
        device_id_type=MESH)

    def ar_copy(step, j, source):
        _, i, mate = groups[step]
        return pltpu.make_async_remote_copy(
            src_ref=arbuf.at[step, i], dst_ref=arbuf.at[step, i], send_sem=ars.at[step, j], recv_sem=arr.at[step, source],
            device_id=mate(j), device_id_type=MESH)

    def ar_send(step, value):
        size, i, _ = groups[step]
        arbuf[step, i] = value
        for j in range(1, size):
            ar_copy(step, j, i).start()

    def ar_sum(step):
        size, i, _ = groups[step]
        for j in range(1, size):
            ar_copy(step, j, lax.rem(i + j, size)).wait_recv()
        total = arbuf[step, 0]
        for j in range(1, size):
            total = total + arbuf[step, j]
        return total

    @pl.when(odd)
    def _():
        arbuf[3, 2] = tile
        up.start()

    def ar_step(step):
        @pl.when(even)
        def _():
            if step == 0:
                up.wait_recv()
                ar_send(0, tile + arbuf[3, 0])
            elif step < 3:
                ar_send(step, ar_sum(step - 1))
            else:
                arbuf[3, 2] = ar_sum(2)
                down.start()

    ar_step(0)

    def finish(f, out):
        FB = 64

        def rows_(i, _):
            s = pl.ds(pl.multiple_of(i * FB, FB), FB)
            d = acc[f, s, :]
            r = rinv[f, s, 0:1]
            unit = raw[f, s, :].astype(F32) * r
            dot = jnp.sum(unit * d, axis=-1, keepdims=True)
            out[0, s, :] = ((d - unit * dot) * r).astype(BF16)
            return 0

        lax.fori_loop(0, ROWS // FB, rows_, 0)

    def finish_flow(f):
        @pl.when(f == 0)
        def _():
            finish(0, o_img)

        @pl.when(f == 1)
        def _():
            finish(1, o_txt)

    finish_flow(N)

    for q in range(4):
        for k in (2 * q, 2 * q + 1):
            pltpu.make_async_remote_copy(
                src_ref=buf.at[N, 2, pl.ds(k * CH, CH)], dst_ref=buf.at[N, 3, pl.ds(k * CH, CH)], send_sem=fas.at[k],
                recv_sem=far_r.at[k], device_id={"blk": far}, device_id_type=MESH).wait_recv()
        item(F, 0, 3, q * 128, 128)
        if q < 3:
            ar_step(q + 1)

    finish_flow(F)

    @pl.when(odd)
    def _():
        down.wait_recv()

    fin = jnp.where(odd, arbuf[3, 1], arbuf[3, 2])
    for i in range(3):
        o_stats[i] = jnp.sum(fin[i:i + 1, :]) / F32(blocks * reps * ROWS)

    def left(k, _):
        z_send(F, k).wait_send()
        fwd_f(k).wait_send()
        fwd_n(k).wait_send()
        far_send(k).wait_send()
        return 0

    lax.fori_loop(0, NCH, left, 0)
    for k in (6, 7):
        z_send(N, k).wait_send()
    for j in range(ROWS // LB):
        peer_send(j).wait_send()
    for r in (1, 2, 3):
        lab_send(r).wait_send()

    @pl.when(odd)
    def _():
        up.wait_send()

    @pl.when(even)
    def _():
        for step in range(3):
            for j in range(1, groups[step][0]):
                ar_copy(step, j, 0).wait_send()
        down.wait_send()


def solution(mesh):
    blocks, reps = mesh.shape["blk"], mesh.shape["rep"]
    hbm = pl.BlockSpec(memory_space=pltpu.HBM)
    vmem = pl.BlockSpec(memory_space=pltpu.VMEM)
    smem = pl.BlockSpec(memory_space=pltpu.SMEM)
    dma = pltpu.SemaphoreType.DMA
    reg = pltpu.SemaphoreType.REGULAR

    def step(images, texts, labels, log_temp, bias):
        shape = (1, ROWS, D)
        return pl.pallas_call(
            functools.partial(kernel, blocks, reps),
            out_shape=(pltpu.VMEM(shape, BF16), pltpu.VMEM(shape, BF16), jax.ShapeDtypeStruct((3,), F32)),
            in_specs=[hbm, hbm, hbm, smem, smem],
            out_specs=(vmem, vmem, smem),
            scratch_shapes=[
                pltpu.VMEM((2, 4, ROWS, D), BF16),
                pltpu.VMEM((2, ROWS, D), BF16),
                pltpu.VMEM((2, ROWS, D), F32),
                pltpu.VMEM((2, ROWS, 128), F32),
                pltpu.VMEM((2, 4, 1, ROWS), jnp.int32),
                pltpu.VMEM((2, ROWS, 128), jnp.int32),
                pltpu.VMEM((2, 1, 256), F32),
                pltpu.VMEM((ROWS, 256), F32),
                pltpu.VMEM((3, 8, 128), F32),
                pltpu.VMEM((4, 8, 8, 128), F32),
                dma((2, 4)), dma,
                dma((2, NCH)), dma((2, NCH)), dma((4,)), dma((4,)),
                dma((NCH,)), dma((NCH,)), dma((NCH,)), dma((NCH,)), dma((NCH,)), dma((NCH,)),
                dma((3,)), dma((3,)),
                dma, dma, dma, dma, dma((3, 8)), dma((3, 8)),
                reg, reg,
            ],
            compiler_params=pltpu.CompilerParams(
                collective_id=0, has_side_effects=True, vmem_limit_bytes=48 * 2**20),
            name="siglip",
        )(images, texts, labels, log_temp, bias)

    return jax.shard_map(
        step,
        mesh=mesh,
        in_specs=(P("rep", "blk", None), P("rep", "blk", None), P("rep", "blk"), P(), P()),
        out_specs=(P("rep", "blk", None), P("rep", "blk", None), P()),
        check_vma=False,
    )
```

time: 341 us -> 95.8 us (0.28)
  blocking collectives: 153 us -> 0 us
  waiting for transfers between devices: 89.5 us -> 0 us
  Pallas kernels: 0 us -> 87.8 us
  matrix products: 36.7 us -> 0 us
  starting transfers between devices: 35.2 us -> 0 us
  other arithmetic: 22.7 us -> 0 us
  local copies, waits for them, and re-layouts: 0.13 us -> 5.75 us
    psum x1 -> x0, blocking collectives: 153 us -> none  [shards(): summed = lax.psum(totals, ('blk', 'rep'))]
    ppermute x7 -> x0, waiting for transfers between devices: 89.5 us -> none  [passed_along(): return lax.ppermute(value, axis, pairs)]
    pallas_call x0 -> x1, Pallas kernels: none -> 87.8 us  [step(): pl.pallas_call(functools.partial(kernel, blocks, reps), out_shape=(pltpu....]
    dot_general x12 -> x0, matrix products: 36.7 us -> none  [the longest x4 13.6 us: block_scores(): lax.dot_general(img_unit, txt_unit, (((1,), (1,)), ((), ())), preferred_e...]
    ppermute x7 -> x0, starting transfers between devices: 35.2 us -> none  [passed_along(): return lax.ppermute(value, axis, pairs)]
    add x7 -> x0, other arithmetic: 15.2 us -> none  [the longest x1 8.21 us: shards(): totals = totals + extra]
    unnamed x38 -> x9, local copies, waits for them, and re-layouts: 0.13 us -> 5.75 us
    reduce_sum x3 -> x0, other arithmetic: 3.75 us -> none  [the longest x2 3.31 us: normalize(): rinv = lax.rsqrt(jnp.sum(rows32 * rows32, axis=-1, keepdims=True) + EPS)]
  transfers between devices with their start and end apart: 7 -> 0, of which waited for: 4 -> 0; matrix products, arithmetic and copies ran while one was open for 12% -> 0% of each run, Pallas kernels for 0% -> 0%
where the time goes in v1:
time: 95.8 us; the launch traced here: 95.5 us
  Pallas kernels  87.8 us (92%)
  local copies, waits for them, and re-layouts  5.75 us (6%)
  between operations  1.94 us (2%)
    pallas_call x1, Pallas kernels, step(): pl.pallas_call(functools.partial(kernel, blocks, reps), out_shape=(pltpu....  87.8 us
    unnamed x9, local copies, waits for them, and re-layouts  5.75 us

profile of v1, /device:TPU:1, one launch (start us, length us, event | category | flops | bytes accessed | tf_op | source)
XLA Modules:
  0.0 95.5 jit_solution(7512643242329041668)
XLA Ops:
  1.9 0.0 copy-start
  1.9 1.3 %copy-done = bf16[1,512,1152]{2,1,0:T(8,128)(2,1)S(1)} copy-done((bf16[1,512,1152]{2,1,0:T(8,128)(2,1)S(1)}, bf16[1,512,1152]{2,1,0:T(8,128)(2,1)}, u32[]{:S(2)}) %copy-start) | copy-done | bytes 1179672
  3.2 0.0 copy-start.1
  3.2 1.3 %copy-done.1 = bf16[1,512,1152]{2,1,0:T(8,128)(2,1)S(1)} copy-done((bf16[1,512,1152]{2,1,0:T(8,128)(2,1)S(1)}, bf16[1,512,1152]{2,1,0:T(8,128)(2,1)}, u32[]{:S(2)}) %copy-start.1) | copy-done | bytes 1179672
  4.5 0.0 copy-start.2
  4.5 0.7 copy-done.2
  5.1 87.8 %siglip.1 = (bf16[1,512,1152]{2,1,0:T(8,128)(2,1)S(1)}, bf16[1,512,1152]{2,1,0:T(8,128)(2,1)S(1)}, f32[3]{0:T(128)S(1)}) custom-call(bf16[1,512,1152]{2,1,0:T(8,128)(2,1)S(1)} %copy-done, bf16[1,512,1152]{2,1,0:T(8,128)(2,1)S(1)} %copy-done.1, s32[1,512]{1,0:T(1,128)S(1)} %copy-done.2, f32[1]{0:T(128)S(6)} %copy.13.log_temp, f32[1]{0:T(128)S(6)} %copy.14.bias), custom_call_target="tpu_custom_call" | custom-call | tf_op jit(solution)/shard_map/siglip/pallas_call | solution.py:417
  92.9 1.0 %copy.11 = bf16[1,512,1152]{2,1,0:T(8,128)(2,1)} copy(bf16[1,512,1152]{2,1,0:T(8,128)(2,1)S(1)} %get-tuple-element.3) | data formatting | bytes 2359296
  93.9 1.0 %copy.12 = bf16[1,512,1152]{2,1,0:T(8,128)(2,1)} copy(bf16[1,512,1152]{2,1,0:T(8,128)(2,1)S(1)} %get-tuple-element.4) | data formatting | bytes 2359296
  95.0 0.5 copy.15
Async XLA Ops:
  1.9 1.3 %copy-start = (bf16[1,512,1152]{2,1,0:T(8,128)(2,1)S(1)}, bf16[1,512,1152]{2,1,0:T(8,128)(2,1)}, u32[]{:S(2)}) copy-start(bf16[1,512,1152]{2,1,0:T(8,128)(2,1)} %images.1) | copy-start | bytes 3538948
  3.2 1.3 %copy-start.1 = (bf16[1,512,1152]{2,1,0:T(8,128)(2,1)S(1)}, bf16[1,512,1152]{2,1,0:T(8,128)(2,1)}, u32[]{:S(2)}) copy-start(bf16[1,512,1152]{2,1,0:T(8,128)(2,1)} %texts.1) | copy-start | bytes 3538948
  4.5 0.7 copy-start.2

commit v2 on v1

v2 whole, which is shorter than its diff:
```python
import functools

import jax
import jax.numpy as jnp
from jax import lax
from jax.experimental import pallas as pl
from jax.experimental.pallas import tpu as pltpu
from jax.sharding import PartitionSpec as P

MESH = pl.DeviceIdType.MESH
EPS = 1e-06
F32 = jnp.float32
BF16 = jnp.bfloat16
ROWS = 512
D = 1152
CH = 64
NCH = ROWS // CH
GO_AT = 5
ZS, YS, XS = 8, 8, 2


def kernel(blocks, reps, images, texts, labels, log_temp, bias, o_img, o_txt, o_stats,
           buf, raw, acc, rinv, rowv, colv, consts, sbuf, st, arbuf,
           ld, ldl, zs, zr, ps, pr, f1s, f1r, f3s, f3r, fas, far_r, ls, lr,
           os_, or_, ars, arr, rdy, go, fargo):
    me = lax.axis_index("blk")
    rep = lax.axis_index("rep")
    core = lax.rem(me, 2)
    F = core
    N = 1 - core
    sgn = 2 * core - 1

    def at(step):
        return lax.rem(me + step + blocks, blocks)

    peer, far = at(-sgn), at(sgn)
    even, odd = core == 0, core == 1
    z = lax.rem(me // 2, ZS)
    y = lax.rem(me // (2 * ZS), YS)
    x = me // (2 * ZS * YS)
    xi = x * reps + rep

    def x_mate(j):
        i = lax.rem(xi + j, XS * reps)
        return {"blk": me + (i // reps - x) * (2 * ZS * YS), "rep": lax.rem(i, reps)}

    def y_mate(j):
        return {"blk": me + (lax.rem(y + j, YS) - y) * (2 * ZS)}

    def z_mate(j):
        return {"blk": me + (lax.rem(z + j, ZS) - z) * 2}

    def z_odd(j):
        return {"blk": me + 1 + (lax.rem(z + j, ZS) - z) * 2}

    groups = [(XS * reps, xi, x_mate), (YS, y, y_mate), (ZS, z, z_mate)]

    bar = pltpu.get_barrier_semaphore()

    def hello(step):
        pl.semaphore_signal(bar, inc=1, device_id={"blk": at(step)}, device_id_type=MESH)

    hello(2)
    hello(-2)

    @pl.when(odd)
    def _():
        for step in (1, -1, 3, -3):
            hello(step)
        for j in range(ZS):
            pl.semaphore_signal(bar, inc=1, device_id={"blk": z_mate(j)["blk"] - 1}, device_id_type=MESH)

    @pl.when(even)
    def _():
        for size, _, mate in groups:
            for j in range(1, size):
                pl.semaphore_signal(bar, inc=1, device_id=mate(j), device_id_type=MESH)

    LB = 128
    srcs = (images, texts)

    def load(f, j):
        s = pl.ds(j * LB, LB)
        return pltpu.make_async_copy(srcs[f].at[0, s], raw.at[f, s], ld.at[f, j])

    for j in range(ROWS // LB):
        for f in (0, 1):
            load(f, j).start()
    lab_load = pltpu.make_async_copy(labels, rowv.at[1, 0], ldl)
    lab_load.start()

    def z_send(f, k):
        s = pl.ds(k * CH, CH)
        return pltpu.make_async_remote_copy(
            src_ref=buf.at[f, 0, s], dst_ref=buf.at[f, 2, s], send_sem=zs.at[f, k], recv_sem=zr.at[f, k],
            device_id={"blk": at(4 * f - 2)}, device_id_type=MESH)

    def peer_send(j):
        s = pl.ds(j * LB, LB)
        return pltpu.make_async_remote_copy(
            src_ref=buf.at[N, 0, s], dst_ref=buf.at[N, 1, s], send_sem=ps.at[j], recv_sem=pr.at[j],
            device_id={"blk": peer}, device_id_type=MESH)

    def pass_on(f, slot_to, k, ss, rs, to):
        s = pl.ds(k * CH, CH)
        return pltpu.make_async_remote_copy(
            src_ref=buf.at[f, 2, s], dst_ref=buf.at[f, slot_to, s], send_sem=ss.at[k], recv_sem=rs.at[k],
            device_id={"blk": to}, device_id_type=MESH)

    def fwd_f(k):
        return pass_on(F, 1, k, f1s, f1r, peer)

    def fwd_n(k):
        return pass_on(N, 3, k, f3s, f3r, peer)

    def far_send(k):
        return pass_on(F, 3, k, fas, far_r, far)

    def far_recv(k):
        return pass_on(N, 3, k, fas, far_r, far)

    def lab_send(r):
        return pltpu.make_async_remote_copy(
            src_ref=rowv.at[1, 0], dst_ref=rowv.at[1, r], send_sem=ls.at[r - 1], recv_sem=lr.at[r - 1],
            device_id={"blk": at(-r)}, device_id_type=MESH)

    def each(lo, hi, fn):
        def step(k, _):
            fn(k)
            return 0

        lax.fori_loop(lo, hi, step, 0)

    for j in range(ROWS // LB):
        for f in (0, 1):
            load(f, j).wait()
            s = slice(j * LB, (j + 1) * LB)
            x32 = raw[f, s, :].astype(F32)
            r = lax.rsqrt(jnp.sum(x32 * x32, axis=-1, keepdims=True) + EPS)
            buf[f, 0, s, :] = (x32 * r).astype(BF16)
            rinv[f, s, :] = jnp.broadcast_to(r, (LB, 128))

        @pl.when(odd)
        def _():
            if j == 0:
                pl.semaphore_wait(bar, 2)
            for k in range(j * LB // CH, (j + 1) * LB // CH):
                for f in (0, 1):
                    z_send(f, k).start()

    lab_load.wait()
    lane = lax.broadcasted_iota(jnp.int32, (1, ROWS), 1)
    for r in range(4):
        rowv[0, r] = lane + at(-r) * ROWS
    colv[0] = jnp.transpose(jnp.broadcast_to(rowv[1, 0].astype(F32), (128, ROWS))).astype(jnp.int32)
    colv[1] = lax.broadcasted_iota(jnp.int32, (ROWS, 128), 0) + me * ROWS
    consts[0] = jnp.exp(jnp.full((1, ROWS), log_temp[0], F32))
    consts[1] = jnp.full((1, ROWS), bias[0], F32)
    st[...] = jnp.zeros_like(st)

    def clear(i):
        for f in (0, 1):
            acc[f, pl.ds(pl.multiple_of(i * 64, 64), 64), :] = jnp.zeros((64, D), F32)

    each(0, ROWS // 64, clear)

    def matches(f, rows, r, c0, width, shift=0):
        ids = colv[f, rows, :]
        ids = jnp.concatenate([ids] * (width // 128), axis=1) if width > 128 else ids
        return ids == rowv[f, r, :, pl.ds(c0, width)] - shift

    def scores(f, own, rb, rows, r, c0, width):
        return consts[0, :, :width] * lax.dot_general(
            buf[f, own, rb:rb + rows, :], buf[1 - f, r, pl.ds(c0, width), :], (((1,), (1,)), ((), ())),
            preferred_element_type=F32)

    def item(f, r, c0, width, keep=False):
        RB = 256
        for rb in range(0, ROWS, RB):
            scaled = scores(f, 0, rb, RB, r, c0, width)
            if keep:
                sbuf[rb:rb + RB, :width] = scaled
            logit = scaled + consts[1, :, :width]
            m = matches(f, slice(rb, rb + RB), r, c0, width)
            sig = 1.0 / (1.0 + jnp.exp(jnp.where(m, logit, -logit)))
            w = (consts[0, :, :width] * jnp.where(m, -sig, sig)).astype(BF16)
            acc[f, rb:rb + RB, :] += jnp.dot(w, buf[1 - f, r, pl.ds(c0, width), :], preferred_element_type=F32)

    def tally(f, r, c0, width, shift=0):
        SB = 64 if width <= 256 else 32

        def rows_(i, tot):
            s = pl.ds(pl.multiple_of(i * SB, SB), SB)
            scaled = sbuf[s, :width]
            logit = scaled + consts[1, :, :width]
            m = matches(f, s, r, c0, width, shift)
            u = jnp.where(m, logit, -logit)
            e = jnp.exp(-jnp.abs(u))
            inv = 1.0 / (1.0 + e)
            sig = jnp.where(u >= 0, e * inv, inv)
            g = jnp.where(m, -sig, sig)
            loss = jnp.maximum(-u, 0.0) + jnp.log1p(e)
            out = []
            for t, v in zip(tot, (loss, g * scaled, g)):
                v = jnp.sum(v.reshape(SB // 8, 8, width), axis=0)
                for c in range(0, width, 128):
                    t = t + v[:, c:c + 128]
                out.append(t)
            return tuple(out)

        tot = lax.fori_loop(0, ROWS // SB, rows_, tuple(jnp.zeros((8, 128), F32) for _ in range(3)))
        for i in range(3):
            st[i] += tot[i]

    def tile():
        row = lax.broadcasted_iota(jnp.int32, (8, 128), 0)
        out = jnp.zeros((8, 128), F32)
        for i in range(3):
            out = jnp.where(row == i, jnp.broadcast_to(jnp.sum(st[i], axis=0, keepdims=True), (8, 128)), out)
        return out

    up = pltpu.make_async_remote_copy(
        src_ref=arbuf.at[3, 1], dst_ref=arbuf.at[3, 0], send_sem=os_, recv_sem=or_, device_id={"blk": peer},
        device_id_type=MESH)

    def ar_copy(step, n, to, source):
        i = groups[step][1]
        return pltpu.make_async_remote_copy(
            src_ref=arbuf.at[step, i], dst_ref=arbuf.at[step, i], send_sem=ars.at[step, n],
            recv_sem=arr.at[step, source], device_id=to, device_id_type=MESH)

    def ar_sends(step):
        size, i, mate = groups[step]
        sends = [ar_copy(step, j - 1, mate(j), i) for j in range(1, size)]
        if step == 2:
            sends += [ar_copy(step, size - 1 + j, z_odd(j), i) for j in range(size)]
        return sends

    def ar_send(step, value):
        arbuf[step, groups[step][1]] = value
        for c in ar_sends(step):
            c.start()

    def ar_sum(step, first=1):
        size, i, mate = groups[step]
        for j in range(first, size):
            ar_copy(step, 0, mate(j) if j else z_odd(0), lax.rem(i + j, size)).wait_recv()
        total = arbuf[step, 0]
        for j in range(1, size):
            total = total + arbuf[step, j]
        return total

    def before_first_near():
        @pl.when(even)
        def _():
            pl.semaphore_wait(bar, 6 + ZS + sum(size - 1 for size, _, _ in groups))
            for step in (1, -1, 3, -3):
                pl.semaphore_signal(rdy, inc=1, device_id={"blk": at(step)}, device_id_type=MESH)

        @pl.when(odd)
        def _():
            pl.semaphore_wait(rdy, 4)

        for j in range(ROWS // LB):
            peer_send(j).start()
        for r in (1, 2, 3):
            lab_send(r).start()
        for j in range(ROWS // LB):
            peer_send(j).wait_recv()
        lab_send(1).wait_recv()

    def both_z(k):
        z_send(0, k).start()
        z_send(1, k).start()

    def both_sent(k):
        z_send(0, k).wait_send()
        z_send(1, k).wait_send()

    def pump(k):
        z_send(F, k).wait_recv()
        fwd_f(k).start()
        z_send(N, k).wait_recv()
        fwd_n(k).start()

    def tell_peer(sem):
        pl.semaphore_signal(sem, inc=1, device_id={"blk": peer}, device_id_type=MESH)

    def before_3():
        @pl.when(odd)
        def _():
            each(0, GO_AT, both_sent)
            tell_peer(go)
            each(0, NCH, pump)

        @pl.when(even)
        def _():
            pl.semaphore_wait(go, 1)
            each(0, NCH, both_z)
            each(0, NCH, lambda k: fwd_f(k).wait_recv())

        for r in (2, 3):
            lab_send(r).wait_recv()

    def before_4():
        @pl.when(odd)
        def _():
            arbuf[3, 1] = tile()
            up.start()

        @pl.when(even)
        def _():
            each(0, NCH, lambda k: fwd_n(k).wait_recv())

    def before_5():
        @pl.when(odd)
        def _():
            pl.semaphore_wait(fargo, 1)
            each(0, NCH, lambda k: far_send(k).start())
            each(0, NCH, lambda k: fwd_f(k).wait_recv())

        @pl.when(even)
        def _():
            def quarter(t):
                q, own = t // 2, lax.rem(t, 2)

                @pl.when(own == 0)
                def _():
                    pump(2 * q)
                    pump(2 * q + 1)

                    @pl.when(q == 1)
                    def _():
                        each(0, GO_AT, both_sent)
                        tell_peer(fargo)

                c0 = pl.multiple_of(q * 128, 128)
                for rb in range(0, ROWS, 256):
                    sbuf[rb:rb + 256, :128] = scores(1, own, rb, 256, 2, c0, 128)
                tally(1, 2, c0, 128, (at(-own) - me) * ROWS)

                @pl.when(jnp.logical_and(own == 1, q >= 1))
                def _():
                    each(jnp.where(q == 1, 0, 2 * q), 2 * q + 2, lambda k: far_send(k).start())

            each(0, 8, quarter)
            up.wait_recv()
            ar_send(0, tile() + arbuf[3, 0])

    def before_6():
        @pl.when(odd)
        def _():
            each(0, NCH, lambda k: fwd_n(k).wait_recv())

    syncs = {2: before_first_near, 3: before_3, 4: before_4, 5: before_5, 6: before_6}

    def pair(i):
        for at_i, sync in syncs.items():
            pl.when(i == at_i)(sync)
        via_peer = jnp.logical_or(jnp.logical_and(i < 5, even), jnp.logical_and(i >= 5, odd))
        second = lax.rem(i, 2) == 0
        late_f = jnp.where(jnp.logical_xor(via_peer, second), F, N)
        f = jnp.where(i == 1, F, jnp.where(i < 3, N, late_f))
        r = jnp.where(i < 2, 0, jnp.where(i == 2, 1, jnp.where(via_peer, jnp.where(second, 3, 1), 2)))
        item(f, r, 0, ROWS, True)
        counted = jnp.where(even, jnp.where(f == 0, r <= 1, r == 3), jnp.logical_and(f == 0, r <= 2))

        @pl.when(counted)
        def _():
            tally(f, r, 0, ROWS)

    each(0, 7, pair)

    def finish(f, out):
        FB = 64

        def rows_(i):
            s = pl.ds(pl.multiple_of(i * FB, FB), FB)
            d = acc[f, s, :]
            r = rinv[f, s, 0:1]
            unit = raw[f, s, :].astype(F32) * r
            dot = jnp.sum(unit * d, axis=-1, keepdims=True)
            out[0, s, :] = ((d - unit * dot) * r).astype(BF16)

        each(0, ROWS // FB, rows_)

    def finish_flow(f):
        @pl.when(f == 0)
        def _():
            finish(0, o_img)

        @pl.when(f == 1)
        def _():
            finish(1, o_txt)

    @pl.when(even)
    def _():
        ar_send(1, ar_sum(0))

    each(0, 4, lambda k: far_recv(k).wait_recv())
    item(F, 3, 0, 256)
    finish_flow(N)

    def last(q):
        for j in (0, 1):
            far_recv(2 * q + j).wait_recv()
        item(F, 3, pl.multiple_of(q * 128, 128), 128)

        @pl.when(jnp.logical_and(even, q == 2))
        def _():
            ar_send(2, ar_sum(1))

    each(2, 4, last)
    finish_flow(F)

    @pl.when(odd)
    def _():
        ar_sum(2, 0)

    @pl.when(even)
    def _():
        ar_sum(2)

    fin = arbuf[2, 0]
    for j in range(1, ZS):
        fin = fin + arbuf[2, j]
    for i in range(3):
        o_stats[i] = jnp.sum(fin[i:i + 1, :]) / F32(blocks * reps * ROWS)

    each(GO_AT, NCH, both_sent)

    def left(k):
        fwd_f(k).wait_send()
        fwd_n(k).wait_send()
        far_send(k).wait_send()

    each(0, NCH, left)
    for j in range(ROWS // LB):
        peer_send(j).wait_send()
    for r in (1, 2, 3):
        lab_send(r).wait_send()

    @pl.when(odd)
    def _():
        up.wait_send()

    @pl.when(even)
    def _():
        for step in range(3):
            for c in ar_sends(step):
                c.wait_send()


def solution(mesh):
    blocks, reps = mesh.shape["blk"], mesh.shape["rep"]
    hbm = pl.BlockSpec(memory_space=pltpu.HBM)
    vmem = pl.BlockSpec(memory_space=pltpu.VMEM)
    smem = pl.BlockSpec(memory_space=pltpu.SMEM)
    dma = pltpu.SemaphoreType.DMA
    reg = pltpu.SemaphoreType.REGULAR

    def step(images, texts, labels, log_temp, bias):
        shape = (1, ROWS, D)
        return pl.pallas_call(
            functools.partial(kernel, blocks, reps),
            out_shape=(pltpu.VMEM(shape, BF16), pltpu.VMEM(shape, BF16), jax.ShapeDtypeStruct((3,), F32)),
            in_specs=[hbm, hbm, hbm, smem, smem],
            out_specs=(vmem, vmem, smem),
            scratch_shapes=[
                pltpu.VMEM((2, 4, ROWS, D), BF16),
                pltpu.VMEM((2, ROWS, D), BF16),
                pltpu.VMEM((2, ROWS, D), F32),
                pltpu.VMEM((2, ROWS, 128), F32),
                pltpu.VMEM((2, 4, 1, ROWS), jnp.int32),
                pltpu.VMEM((2, ROWS, 128), jnp.int32),
                pltpu.VMEM((2, 1, ROWS), F32),
                pltpu.VMEM((ROWS, ROWS), F32),
                pltpu.VMEM((3, 8, 128), F32),
                pltpu.VMEM((4, 8, 8, 128), F32),
                dma((2, 4)), dma,
                dma((2, NCH)), dma((2, NCH)), dma((4,)), dma((4,)),
                dma((NCH,)), dma((NCH,)), dma((NCH,)), dma((NCH,)), dma((NCH,)), dma((NCH,)),
                dma((3,)), dma((3,)),
                dma, dma, dma((3, 16)), dma((3, 8)),
                reg, reg, reg,
            ],
            compiler_params=pltpu.CompilerParams(
                collective_id=0, has_side_effects=True, vmem_limit_bytes=48 * 2**20),
            name="siglip",
        )(*[pltpu.with_memory_space_constraint(v, pltpu.HBM) for v in (images, texts, labels)], log_temp, bias)

    return jax.shard_map(
        step,
        mesh=mesh,
        in_specs=(P("rep", "blk", None), P("rep", "blk", None), P("rep", "blk"), P(), P()),
        out_specs=(P("rep", "blk", None), P("rep", "blk", None), P()),
        check_vma=False,
    )
```

time: 95.8 us -> 65.9 us (0.69)
  Pallas kernels: 87.8 us -> 61.3 us
  local copies, waits for them, and re-layouts: 5.75 us -> 2.54 us
    pallas_call x1, Pallas kernels: 87.8 us -> 61.3 us  [step(): pl.pallas_call(functools.partial(kernel, blocks, reps), out_shape=(pltpu....]
    unnamed x9 -> x3, local copies, waits for them, and re-layouts: 5.75 us -> 2.54 us
where the time goes in v2:
time: 65.9 us; the launch traced here: 65.8 us
  Pallas kernels  61.3 us (93%)
  local copies, waits for them, and re-layouts  2.54 us (4%)
  between operations  1.93 us (3%)
    pallas_call x1, Pallas kernels, step(): pl.pallas_call(functools.partial(kernel, blocks, reps), out_shape=(pltpu....  61.3 us
    unnamed x3, local copies, waits for them, and re-layouts  2.54 us

profile of v2, /device:TPU:1, one launch (start us, length us, event | category | flops | bytes accessed | tf_op | source)
XLA Modules:
  0.0 65.8 jit_solution(6591890369813649113)
XLA Ops:
  1.9 61.3 %siglip.1 = (bf16[1,512,1152]{2,1,0:T(8,128)(2,1)S(1)}, bf16[1,512,1152]{2,1,0:T(8,128)(2,1)S(1)}, f32[3]{0:T(128)S(1)}) custom-call(bf16[1,512,1152]{2,1,0:T(8,128)(2,1)} %images.1, bf16[1,512,1152]{2,1,0:T(8,128)(2,1)} %texts.1, s32[1,512]{1,0:T(1,128)} %labels.1, f32[1]{0:T(128)S(6)} %copy.13.log_temp, f32[1]{0:T(128)S(6)} %copy.14.bias), custom_call_target="tpu_custom_call" | custom-call | tf_op jit(solution)/shard_map/siglip/pallas_call | solution.py:464
  63.2 1.0 %copy.11 = bf16[1,512,1152]{2,1,0:T(8,128)(2,1)} copy(bf16[1,512,1152]{2,1,0:T(8,128)(2,1)S(1)} %get-tuple-element.3) | data formatting | bytes 2359296
  64.3 1.0 %copy.12 = bf16[1,512,1152]{2,1,0:T(8,128)(2,1)} copy(bf16[1,512,1152]{2,1,0:T(8,128)(2,1)S(1)} %get-tuple-element.4) | data formatting | bytes 2359296
  65.3 0.5 copy.15

commit v3 on v2

--- a/solution.py
+++ b/solution.py
@@ -55,27 +55,6 @@
 
     groups = [(XS * reps, xi, x_mate), (YS, y, y_mate), (ZS, z, z_mate)]
 
-    bar = pltpu.get_barrier_semaphore()
-
-    def hello(step):
-        pl.semaphore_signal(bar, inc=1, device_id={"blk": at(step)}, device_id_type=MESH)
-
-    hello(2)
-    hello(-2)
-
-    @pl.when(odd)
-    def _():
-        for step in (1, -1, 3, -3):
-            hello(step)
-        for j in range(ZS):
-            pl.semaphore_signal(bar, inc=1, device_id={"blk": z_mate(j)["blk"] - 1}, device_id_type=MESH)
-
-    @pl.when(even)
-    def _():
-        for size, _, mate in groups:
-            for j in range(1, size):
-                pl.semaphore_signal(bar, inc=1, device_id=mate(j), device_id_type=MESH)
-
     LB = 128
     srcs = (images, texts)
 
@@ -88,6 +67,14 @@
             load(f, j).start()
     lab_load = pltpu.make_async_copy(labels, rowv.at[1, 0], ldl)
     lab_load.start()
+
+    bar = pltpu.get_barrier_semaphore()
+
+    def hello(step):
+        pl.semaphore_signal(bar, inc=1, device_id={"blk": at(step)}, device_id_type=MESH)
+
+    hello(2)
+    hello(-2)
 
     def z_send(f, k):
         s = pl.ds(k * CH, CH)
@@ -147,6 +134,19 @@
             for k in range(j * LB // CH, (j + 1) * LB // CH):
                 for f in (0, 1):
                     z_send(f, k).start()
+
+    @pl.when(odd)
+    def _():
+        for step in (1, -1, 3, -3):
+            hello(step)
+        for j in range(ZS):
+            pl.semaphore_signal(bar, inc=1, device_id={"blk": z_mate(j)["blk"] - 1}, device_id_type=MESH)
+
+    @pl.when(even)
+    def _():
+        for size, _, mate in groups:
+            for j in range(1, size):
+                pl.semaphore_signal(bar, inc=1, device_id=mate(j), device_id_type=MESH)
 
     lab_load.wait()
     lane = lax.broadcasted_iota(jnp.int32, (1, ROWS), 1)
@@ -451,6 +451,14 @@
                 c.wait_send()
 
 
+def write_out(a, b, out_a, out_b, sems):
+    copies = [pltpu.make_async_copy(v, o, sems.at[i]) for i, (v, o) in enumerate(((a, out_a), (b, out_b)))]
+    for copy in copies:
+        copy.start()
+    for copy in copies:
+        copy.wait()
+
+
 def solution(mesh):
     blocks, reps = mesh.shape["blk"], mesh.shape["rep"]
     hbm = pl.BlockSpec(memory_space=pltpu.HBM)
@@ -461,7 +469,7 @@
 
     def step(images, texts, labels, log_temp, bias):
         shape = (1, ROWS, D)
-        return pl.pallas_call(
+        *grads, stats = pl.pallas_call(
             functools.partial(kernel, blocks, reps),
             out_shape=(pltpu.VMEM(shape, BF16), pltpu.VMEM(shape, BF16), jax.ShapeDtypeStruct((3,), F32)),
             in_specs=[hbm, hbm, hbm, smem, smem],
@@ -489,6 +497,18 @@
             name="siglip",
         )(*[pltpu.with_memory_space_constraint(v, pltpu.HBM) for v in (images, texts, labels)], log_temp, bias)
 
+        full = jax.ShapeDtypeStruct(shape, BF16)
+        anywhere = pl.BlockSpec(memory_space=pl.ANY)
+        written = pl.pallas_call(
+            write_out,
+            out_shape=(full, full),
+            in_specs=[anywhere] * 2,
+            out_specs=(hbm, hbm),
+            scratch_shapes=[dma((2,))],
+            name="write_out",
+        )(*[pltpu.with_memory_space_constraint(v, pltpu.VMEM) for v in grads])
+        return *written, stats
+
     return jax.shard_map(
         step,
         mesh=mesh,

time: 65.9 us -> 65.2 us (0.989)
  local copies, waits for them, and re-layouts: 2.54 us -> 0.51 us
  Pallas kernels: 61.3 us -> 62.6 us
    unnamed x3 -> x1, local copies, waits for them, and re-layouts: 2.54 us -> 0.51 us
    pallas_call x0 -> x1, Pallas kernels: none -> 1.42 us  [step(): pl.pallas_call(write_out, out_shape=(full, full), in_specs=[anywhere] * 2...]
where the time goes in v3:
time: 65.2 us; the launch traced here: 65 us
  Pallas kernels  62.6 us (96%)
  between operations  1.94 us (3%)
    pallas_call x1, Pallas kernels, step(): pl.pallas_call(functools.partial(kernel, blocks, reps), out_shape=(pltpu....  61.2 us
    pallas_call x1, Pallas kernels, step(): pl.pallas_call(write_out, out_shape=(full, full), in_specs=[anywhere] * 2...  1.42 us

profile of v3, /device:TPU:1, one launch (start us, length us, event | category | flops | bytes accessed | tf_op | source)
XLA Modules:
  0.0 65.0 jit_solution(10117369910781878687)
XLA Ops:
  1.9 61.2 %siglip.1 = (bf16[1,512,1152]{2,1,0:T(8,128)(2,1)S(1)}, bf16[1,512,1152]{2,1,0:T(8,128)(2,1)S(1)}, f32[3]{0:T(128)S(1)}) custom-call(bf16[1,512,1152]{2,1,0:T(8,128)(2,1)} %images.1, bf16[1,512,1152]{2,1,0:T(8,128)(2,1)} %texts.1, s32[1,512]{1,0:T(1,128)} %labels.1, f32[1]{0:T(128)S(6)} %copy.9.log_temp, f32[1]{0:T(128)S(6)} %copy.10.bias), custom_call_target="tpu_custom_call" | custom-call | tf_op jit(solution)/shard_map/siglip/pallas_call | solution.py:472
  63.1 1.4 %write_out.1 = (bf16[1,512,1152]{2,1,0:T(8,128)(2,1)}, bf16[1,512,1152]{2,1,0:T(8,128)(2,1)}) custom-call(bf16[1,512,1152]{2,1,0:T(8,128)(2,1)S(1)} %get-tuple-element.8.a, bf16[1,512,1152]{2,1,0:T(8,128)(2,1)S(1)} %get-tuple-element.9.b), custom_call_target="tpu_custom_call" | custom-call | tf_op jit(solution)/shard_map/write_out/pallas_call | solution.py:502
  64.5 0.5 copy.11

commit v4 on v3

--- a/solution.py
+++ b/solution.py
@@ -402,13 +402,13 @@
     finish_flow(N)
 
     def last(q):
+        @pl.when(jnp.logical_and(even, q == 2))
+        def _():
+            ar_send(2, ar_sum(1))
+
         for j in (0, 1):
             far_recv(2 * q + j).wait_recv()
         item(F, 3, pl.multiple_of(q * 128, 128), 128)
-
-        @pl.when(jnp.logical_and(even, q == 2))
-        def _():
-            ar_send(2, ar_sum(1))
 
     each(2, 4, last)
     finish_flow(F)

time: 65.2 us -> 65.6 us (level)
  no operation moved by 1% of the time
where the time goes in v4:
time: 65.6 us; the launch traced here: 65 us
  Pallas kernels  62.6 us (95%)
  between operations  1.94 us (3%)
    pallas_call x1, Pallas kernels, step(): pl.pallas_call(functools.partial(kernel, blocks, reps), out_shape=(pltpu....  61.2 us
    pallas_call x1, Pallas kernels, step(): pl.pallas_call(write_out, out_shape=(full, full), in_specs=[anywhere] * 2...  1.42 us

profile of v4, /device:TPU:1, one launch (start us, length us, event | category | flops | bytes accessed | tf_op | source)
XLA Modules:
  0.0 65.0 jit_solution(14646458395881125597)
XLA Ops:
  1.9 61.2 %siglip.1 = (bf16[1,512,1152]{2,1,0:T(8,128)(2,1)S(1)}, bf16[1,512,1152]{2,1,0:T(8,128)(2,1)S(1)}, f32[3]{0:T(128)S(1)}) custom-call(bf16[1,512,1152]{2,1,0:T(8,128)(2,1)} %images.1, bf16[1,512,1152]{2,1,0:T(8,128)(2,1)} %texts.1, s32[1,512]{1,0:T(1,128)} %labels.1, f32[1]{0:T(128)S(6)} %copy.9.log_temp, f32[1]{0:T(128)S(6)} %copy.10.bias), custom_call_target="tpu_custom_call" | custom-call | tf_op jit(solution)/shard_map/siglip/pallas_call | solution.py:472
  63.1 1.4 %write_out.1 = (bf16[1,512,1152]{2,1,0:T(8,128)(2,1)}, bf16[1,512,1152]{2,1,0:T(8,128)(2,1)}) custom-call(bf16[1,512,1152]{2,1,0:T(8,128)(2,1)S(1)} %get-tuple-element.8.a, bf16[1,512,1152]{2,1,0:T(8,128)(2,1)S(1)} %get-tuple-element.9.b), custom_call_target="tpu_custom_call" | custom-call | tf_op jit(solution)/shard_map/write_out/pallas_call | solution.py:502
  64.5 0.5 copy.11
